TPU v7x, 512 devices: a whole 4x4x16 slice. The times are simulated.
512 devices in a mesh: row: 16 (over z), space: 32 (over y, x, core).
Axes of the slice: x: 4, y: 4, z: 16, core: 2. Of those that a mesh axis runs over, the one named last changes fastest.
Arguments:
- features: bfloat16 [8192, 128], P(('row', 'space')), may hold values from -6 to 6
- positions: float32 [3, 8192], P(None, ('row', 'space')), may hold values from -0.5 to 78, as said below
- species: int32 [8192], P(('row', 'space')), may hold values from 0 to 3
- ghost_list: int32 [16, 1024, 32], P('row', 'space'), may hold values from 0 to 15
- edge_recv: int32 [262144], P(('row', 'space')), may hold values from 0 to 16, as said below
- edge_send: int32 [262144], P(('row', 'space')), may hold values from 0 to 1039
- edge_vec: float32 [3, 262144], P(None, ('row', 'space')), may hold values from -5.8 to 5.8, as said below
- w_msg: bfloat16 [128, 256], replicated, may hold values from -0.5 to 0.5
- w_rad1: float32 [8, 128], replicated, may hold values from -2 to 2
- w_rad2: bfloat16 [128, 256], replicated, may hold values from -0.5 to 0.5
- w_up: bfloat16 [256, 128], replicated, may hold values from -0.375 to 0.375
- w_out: float32 [128], replicated, may hold values from -0.5 to 0.5
- hardness: float32 [4], replicated, may hold values from 2 to 4
- width: float32 [4], replicated, may hold values from 0.8 to 1.6
- chi_shift: float32 [4], replicated, may hold values from -1 to 1
- field: float32 [1], replicated, may hold values from 0.01 to 0.03
Outputs:
- new_features: bfloat16 [8192, 128], P(('row', 'space'))
- charges: float32 [8192], P(('row', 'space'))
- forces: float32 [3, 8192], P(None, ('row', 'space'))
- virial: float32 [6, 8192], P(None, ('row', 'space'))
Inputs may be any that keep to these rules, and one draw needn't show every extreme that they name: `edge_recv`: in every domain the edges are ordered by receiver; the slots in use fill the first whole blocks of 128 rows, a quarter of the blocks or more, and the other slots hold 16; some domain uses all its slots. `positions`: every two atoms are 1.5 or more apart. `edge_vec`: each edge's length lies between 1.2 and 5.8.
All inputs are finite; a program needn't handle non-finite values.
Results may differ from a plain program's by a relative error of at most 0.0045.
Values may be sent and summed in bfloat16 or wider, within the bound.
A program may use at most 64 MiB of HBM per device.

v0:
```python
import math
import jax
import jax.numpy as jnp
from jax import lax
from jax.sharding import PartitionSpec as P

ITERS = 2
cutoff = 6.0
message_scale = 0.125
two_over_root_pi = 2.0 / math.sqrt(math.pi)
inverse_root_pi = 1.0 / math.sqrt(math.pi)
pair_limit = 262144


def lookup(species, table):
    result = jnp.zeros(species.shape, jnp.float32)
    for kind in range(table.shape[0]):
        result = result + jnp.where(species == kind, table[kind], 0.0)
    return result


def pair_block(target, target_labels, source, source_labels, source_charge, forces):
    delta = target[:3, :, None] - source[:3, None, :]
    squared = jnp.sum(delta * delta, axis=0)
    same = target_labels[:, None] == source_labels[None, :]
    squared = jnp.where(same, 1.0, squared)
    inverse = lax.rsqrt(squared)
    radius = squared * inverse
    spread = target[3][:, None] * target[3][:, None] + source[3][None, :] * source[3][None, :]
    scale = lax.rsqrt(2.0 * spread)
    scaled = radius * scale
    smear = lax.erf(scaled)
    if forces:
        slope = (
            two_over_root_pi * scale * jnp.exp(-scaled * scaled) * inverse
            - smear * inverse * inverse
        )
        weight = jnp.where(same, 0.0, source_charge[None, :] * slope * inverse)
        first = jnp.sum(weight[None] * delta, axis=2)
        pairs = ((0, 0), (1, 1), (2, 2), (0, 1), (0, 2), (1, 2))
        second = jnp.stack(
            [jnp.sum(weight * delta[left] * delta[right], axis=1) for left, right in pairs]
        )
        return jnp.concatenate([first, second], axis=0)
    kernel = jnp.where(same, 0.0, smear * inverse)
    return jnp.sum(kernel * source_charge[None, :], axis=1)


def pair_sums(target, target_labels, source, source_labels, source_charge, forces):
    count = target.shape[1]
    extent = source.shape[1]
    block = extent
    while block * count > pair_limit and block % 2 == 0:
        block = block // 2
    turns = extent // block
    source_blocks = source.reshape(4, turns, block).transpose(1, 0, 2)
    label_blocks = source_labels.reshape(turns, block)
    charge_blocks = source_charge.reshape(turns, block)
    start_value = jnp.zeros((9, count) if forces else (count,), jnp.float32)

    def accumulate(carry, item):
        return (carry + pair_block(target, target_labels, item[0], item[1], item[2], forces), None)

    total, _ = lax.scan(accumulate, start_value, (source_blocks, label_blocks, charge_blocks))
    return total


def edge_terms(receive, sender_rows, vectors, projected, w_rad1, w_rad2, atoms):
    length = jnp.sqrt(jnp.sum(vectors * vectors, axis=0))
    unit = vectors / length
    order = jnp.arange(1, w_rad1.shape[0] + 1, dtype=jnp.int32).astype(jnp.float32)[:, None]
    ratio = length / cutoff
    envelope = (1.0 - ratio * ratio) * (1.0 - ratio * ratio)
    basis = jnp.sin(order * math.pi * ratio) / ratio * envelope
    mixed = lax.dot_general(
        basis, w_rad1, (((0,), (0,)), ((), ())), precision=lax.Precision.HIGHEST
    )
    radial = jax.nn.silu(mixed).astype(jnp.bfloat16)
    filters = jnp.dot(radial, w_rad2, preferred_element_type=jnp.float32)
    picked = jnp.take(projected, sender_rows, axis=0).astype(jnp.float32) * filters
    chans = w_rad1.shape[1]
    scalar = picked[:, :chans]
    carried = picked[:, chans:]
    joined = [
        scalar,
        unit[0][:, None] * carried,
        unit[1][:, None] * carried,
        unit[2][:, None] * carried,
    ]
    message = jnp.concatenate(joined, axis=1).astype(jnp.bfloat16)
    onehot = (jnp.arange(atoms, dtype=jnp.int32)[:, None] == receive[None, :]).astype(jnp.bfloat16)
    return jnp.dot(onehot, message, preferred_element_type=jnp.float32)


def shards(
    features,
    positions,
    species,
    ghost_list,
    edge_recv,
    edge_send,
    edge_vec,
    w_msg,
    w_rad1,
    w_rad2,
    w_up,
    w_out,
    hardness,
    width,
    chi_shift,
    field,
):
    atoms = features.shape[0]
    chans = features.shape[1]
    lanes = lax.axis_size("space")
    row_at = lax.axis_index("row")
    space_at = lax.axis_index("space")
    lists = ghost_list[0]
    outgoing = jnp.take(features, lists.reshape(-1), axis=0).reshape(lanes, lists.shape[1], chans)
    ghost_rows = jnp.einsum(
        "dkc,cf->dkf",
        lax.all_to_all(outgoing, "space", split_axis=0, concat_axis=0, tiled=True),
        w_msg,
        preferred_element_type=jnp.float32,
    ).astype(jnp.bfloat16)
    own_rows = jnp.dot(features, w_msg, preferred_element_type=jnp.float32).astype(jnp.bfloat16)
    projected = jnp.concatenate([own_rows, ghost_rows.reshape(-1, 2 * chans)], axis=0)
    summed = edge_terms(edge_recv, edge_send, edge_vec, projected, w_rad1, w_rad2, atoms)
    summed = summed * message_scale
    vector_part = summed[:, chans:].reshape(atoms, 3, chans)
    invariant = jnp.concatenate(
        [summed[:, :chans], jnp.sum(vector_part * vector_part, axis=1)], axis=1
    ).astype(jnp.bfloat16)
    hidden = jax.nn.silu(jnp.dot(invariant, w_up, preferred_element_type=jnp.float32))
    new_features = (features.astype(jnp.float32) + hidden).astype(jnp.bfloat16)
    chi = jnp.dot(hidden, w_out, precision=lax.Precision.HIGHEST) + lookup(species, chi_shift)
    sigma = lookup(species, width)
    diag = lookup(species, hardness) + inverse_root_pi / sigma
    placed = jnp.concatenate([positions, sigma[None, :]], axis=0)
    own_labels = (row_at * lanes + space_at) * atoms + jnp.arange(atoms, dtype=jnp.int32)
    everyone = lax.all_gather(placed, ("row", "space"), axis=1, tiled=True)
    all_labels = jnp.arange(everyone.shape[1], dtype=jnp.int32)

    def spread_out(vector):
        return lax.all_gather(vector, ("row", "space"), axis=0, tiled=True)

    rhs = field[0] * positions[2] - chi
    charges = jnp.zeros_like(rhs)
    residual = rhs

    def squares(current):
        return lax.psum(jnp.sum(current * current), ("row", "space"))

    direction = residual
    norm_now = squares(residual)
    for step in range(ITERS):
        image = diag * direction + pair_sums(
            placed, own_labels, everyone, all_labels, spread_out(direction), False
        )
        alpha = norm_now / lax.psum(jnp.sum(direction * image), ("row", "space"))
        charges = charges + alpha * direction
        residual = residual - alpha * image
        fresh = squares(residual)
        direction = residual + fresh / norm_now * direction
        norm_now = fresh
    sums = pair_sums(placed, own_labels, everyone, all_labels, spread_out(charges), True)
    pull = -charges[None, :] * sums[:3]
    forces = jnp.concatenate([pull[:2], pull[2:] + (charges * field[0])[None, :]], axis=0)
    virial = 0.5 * charges[None, :] * sums[3:]
    return (new_features, charges, forces, virial)


def solution(mesh):
    return jax.shard_map(
        shards,
        mesh=mesh,
        in_specs=(
            P(("row", "space"), None),
            P(None, ("row", "space")),
            P(("row", "space")),
            P("row", "space", None),
            P(("row", "space")),
            P(("row", "space")),
            P(None, ("row", "space")),
            P(),
            P(),
            P(),
            P(),
            P(),
            P(),
            P(),
            P(),
            P(),
        ),
        out_specs=(
            P(("row", "space"), None),
            P(("row", "space")),
            P(None, ("row", "space")),
            P(None, ("row", "space")),
        ),
        check_vma=False,
    )
```

profile of v0, /device:TPU:1, one launch (start us, length us, event | category | flops | bytes accessed | tf_op | source)
XLA Modules:
  0.0 782.4 jit_solution(4420758810562936162)
XLA Ops:
  0.6 0.8 reshape_squeeze.6
  1.5 0.7 compare_and_fusion
  2.3 3.6 gather_fusion
  5.9 0.9 broadcast_select_fusion
  6.8 10.4 %all-to-all-start = ((bf16[32,32,128]{2,1,0:T(8,128)(2,1)}), bf16[32,32,128]{2,1,0:T(8,128)(2,1)S(1)}, u32[]{:S(2)}, u32[]{:S(2)}) async-start(bf16[32,32,128]{2,1,0:T(8,128)(2,1)} %broadcast_select_fusion), calls=%async_computation | async-start | bytes 524288 | tf_op jit(solution)/shard_map/all_to_all | solution.py:122
  18.0 0.7 fusion.42
  18.7 0.7 fusion.43
  20.1 2.5 fusion.39
  22.7 138.5 %all-gather = f32[512,16,4]{1,2,0:T(4,128)S(1)} all-gather(f32[1,16,4]{1,2,0:T(4,128)S(1)} %maximum_bitcast_fusion), channel_id=1, replica_groups=mesh['row'=16,'space'=32] {'row','space'}, dimensions={0}, use_global_device_ids=true | all-gather | bytes 131328 | tf_op jit(solution)/shard_map/all_gather | solution.py:141
  161.9 0.7 multiply_convert_fusion.3
  163.2 2.0 gather_fusion.1
  165.3 1.1 convolution_multiply_fusion
  167.3 0.7 add_convert_fusion
  168.0 2.6 fusion.1
  170.9 100.5 %all-reduce = f32[8192]{0:T(1024)S(1)} all-reduce(f32[8192]{0:T(1024)S(1)} %dynamic-update-slice), channel_id=1, replica_groups=mesh['row'=16,'space'=32] {'row','space'}, use_global_device_ids=true, to_apply=%add | all-reduce | flops 8192 | bytes 65536
  271.9 3.2 multiply_reduce_fusion.12
  275.1 99.4 %all-reduce.3 = (f32[]{:T(128)}, f32[]{:T(128)}) all-reduce(f32[]{:T(128)} %get-tuple-element.67, f32[]{:T(128)} %get-tuple-element.66), channel_id=1, replica_groups=mesh['row'=16,'space'=32] {'row','space'}, use_global_device_ids=true, to_apply=%region_3.4 | all-reduce | flops 2 | bytes 16 | tf_op jit(solution)/shard_map/psum | solution.py:152
  375.8 0.6 multiply_reduce_fusion.11
  376.4 99.4 %psum.30 = f32[]{:T(128)} all-reduce(f32[]{:T(128)} %get-tuple-element.83), channel_id=1, replica_groups=mesh['row'=16,'space'=32] {'row','space'}, use_global_device_ids=true, to_apply=%region_9.10 | all-reduce | flops 1 | bytes 8 | tf_op jit(solution)/shard_map/psum | solution.py:152
  477.2 100.3 %all-reduce.1 = f32[8192]{0:T(1024)S(1)} all-reduce(f32[8192]{0:T(1024)S(1)} %get-tuple-element.81), channel_id=1, replica_groups=mesh['row'=16,'space'=32] {'row','space'}, use_global_device_ids=true, to_apply=%add.1 | all-reduce | flops 8192 | bytes 65536
  577.9 0.6 multiply_reduce_fusion.10
  578.5 99.4 %psum.31 = f32[]{:T(128)} all-reduce(f32[]{:T(128)} %multiply_reduce_fusion.10), channel_id=1, replica_groups=mesh['row'=16,'space'=32] {'row','space'}, use_global_device_ids=true, to_apply=%region_12.13 | all-reduce | flops 1 | bytes 8 | tf_op jit(solution)/shard_map/psum | solution.py:160
  679.6 100.3 %all-reduce.2 = f32[8192]{0:T(1024)S(1)} all-reduce(f32[8192]{0:T(1024)S(1)} %dynamic-update-slice.2), channel_id=1, replica_groups=mesh['row'=16,'space'=32] {'row','space'}, use_global_device_ids=true, to_apply=%add.2 | all-reduce | flops 8192 | bytes 65536
  779.8 0.9 multiply_reduce_fusion.2
  (76 shorter events, 6.1 us)
Async XLA Ops:
  0.6 19.3 %copy-start = (bf16[128,256]{1,0:T(8,128)(2,1)S(1)}, bf16[128,256]{1,0:T(8,128)(2,1)}, u32[]{:S(2)}) copy-start(bf16[128,256]{1,0:T(8,128)(2,1)} %param.23) | copy-start | bytes 196612
  2.2 15.0 %copy-start.5 = (s32[512]{0:T(512)S(1)}, s32[512]{0:T(512)}, u32[]{:S(2)}) copy-start(s32[512]{0:T(512)} %param.21) | copy-start | bytes 6148
  2.2 15.7 %copy-start.3 = (f32[3,512]{1,0:T(4,128)S(1)}, f32[3,512]{1,0:T(4,128)}, u32[]{:S(2)}) copy-start(f32[3,512]{1,0:T(4,128)} %param.22) | copy-start | bytes 18436
  2.2 15.8 %copy-start.6 = (f32[4]{0:T(128)S(1)}, f32[4]{0:T(128)}, u32[]{:S(2)}) copy-start(f32[4]{0:T(128)} %param.28) | copy-start | bytes 52
  2.3 16.4 %copy-start.7 = (f32[4]{0:T(128)S(1)}, f32[4]{0:T(128)}, u32[]{:S(2)}) copy-start(f32[4]{0:T(128)} %param.29) | copy-start | bytes 52
  2.3 17.1 %copy-start.8 = (f32[4]{0:T(128)S(1)}, f32[4]{0:T(128)}, u32[]{:S(2)}) copy-start(f32[4]{0:T(128)} %param.30) | copy-start | bytes 52
  2.3 17.7 %copy-start.1 = (bf16[16,128]{1,0:T(8,128)(2,1)S(1)}, bf16[16,128]{1,0:T(8,128)(2,1)}, u32[]{:S(2)}) copy-start(bf16[16,128]{1,0:T(8,128)(2,1)} %param.16) | copy-start | bytes 12292
  2.3 17.8 %copy-start.9 = (s32[16]{0:T(128)S(1)}, s32[16]{0:T(128)}, u32[]{:S(2)}) copy-start(s32[16]{0:T(128)} %param.18) | copy-start | bytes 196
  2.3 20.4 %copy-start.4 = (f32[3,16]{1,0:T(4,128)S(1)}, f32[3,16]{1,0:T(4,128)}, u32[]{:S(2)}) copy-start(f32[3,16]{1,0:T(4,128)} %param.17) | copy-start | bytes 580
  6.8 156.0 %all-to-all-start = ((bf16[32,32,128]{2,1,0:T(8,128)(2,1)}), bf16[32,32,128]{2,1,0:T(8,128)(2,1)S(1)}, u32[]{:S(2)}, u32[]{:S(2)}) async-start(bf16[32,32,128]{2,1,0:T(8,128)(2,1)} %broadcast_select_fusion), calls=%async_computation | async-start | bytes 524288 | tf_op jit(solution)/shard_map/all_to_all | solution.py:122
  161.2 0.7 copy-start.12
  165.1 1.4 copy-start.13
  166.4 0.8 copy-start.2
  166.4 1.6 copy-start.10
  166.4 1.6 copy-start.14
  679.3 101.9 %copy-start.11 = (f32[16]{0:T(128)}, f32[16]{0:T(128)S(1)}, u32[]{:S(2)}) copy-start(f32[16]{0:T(128)S(1)} %get-tuple-element.71) | copy-start | bytes 196
where the time goes:
time: 784 us; the launch traced here: 782 us
  blocking collectives  738 us (94%)
  other arithmetic  12.5 us (2%)
  starting transfers between devices  10.4 us (1%)
  local copies, waits for them, and re-layouts  10.2 us (1%)
    unnamed x3, blocking collectives  301 us
    psum x2, blocking collectives, squares(): return lax.psum(jnp.sum(current * current), ('row', 'space'))  199 us
    all_gather x1, blocking collectives, shards(): everyone = lax.all_gather(placed, ('row', 'space'), axis=1, tiled=True)  138 us
    psum x1, blocking collectives, shards(): alpha = norm_now / lax.psum(jnp.sum(direction * image), ('row', 'space'))  99.4 us
  transfers between devices with their start and end apart: 1, of which 0 were waited for; matrix products, arithmetic and copies ran while one was open for 1% of the time, Pallas kernels for 0%

commit v1 on v0

--- a/solution.py
+++ b/solution.py
@@ -138,7 +138,12 @@
     diag = lookup(species, hardness) + inverse_root_pi / sigma
     placed = jnp.concatenate([positions, sigma[None, :]], axis=0)
     own_labels = (row_at * lanes + space_at) * atoms + jnp.arange(atoms, dtype=jnp.int32)
-    everyone = lax.all_gather(placed, ("row", "space"), axis=1, tiled=True)
+    everyone = jnp.concatenate(
+        lax.all_to_all(
+            jnp.stack([placed] * lax.axis_size(("row", "space"))), ("row", "space"), 0, 0
+        ),
+        axis=1,
+    )
     all_labels = jnp.arange(everyone.shape[1], dtype=jnp.int32)
 
     def spread_out(vector):

time: 784 us -> 680 us (0.87)
  blocking collectives: 738 us -> 612 us
  starting transfers between devices: 10.4 us -> 28.9 us
    all_gather x1 -> x0, blocking collectives: 138 us -> none  [shards(): everyone = lax.all_gather(placed, ('row', 'space'), axis=1, tiled=True)]
    all_to_all x0 -> x1, starting transfers between devices: none -> 18.5 us  [shards(): lax.all_to_all(jnp.stack([placed] * lax.axis_size(('row', 'space'))), ('r...]
    unnamed x3, blocking collectives: 301 us -> 312 us
  transfers between devices with their start and end apart: 1 -> 2, of which waited for: 0 -> 1; matrix products, arithmetic and copies ran while one was open for 1% -> 2% of each run, Pallas kernels for 0% -> 0%
where the time goes in v1:
time: 680 us; the launch traced here: 679 us
  blocking collectives  612 us (90%)
  starting transfers between devices  28.9 us (4%)
  other arithmetic  13.2 us (2%)
  local copies, waits for them, and re-layouts  11.4 us (2%)
    unnamed x3, blocking collectives  312 us
    psum x2, blocking collectives, squares(): return lax.psum(jnp.sum(current * current), ('row', 'space'))  200 us
    psum x1, blocking collectives, shards(): alpha = norm_now / lax.psum(jnp.sum(direction * image), ('row', 'space'))  99.7 us
    all_to_all x1, starting transfers between devices, shards(): lax.all_to_all(jnp.stack([placed] * lax.axis_size(('row', 'space'))), ('r...  18.5 us
  transfers between devices with their start and end apart: 2, of which 1 were waited for; matrix products, arithmetic and copies ran while one was open for 2% of the time, Pallas kernels for 0%

profile of v1, /device:TPU:1, one launch (start us, length us, event | category | flops | bytes accessed | tf_op | source)
XLA Modules:
  0.0 678.8 jit_solution(423173605246122401)
XLA Ops:
  0.6 0.8 reshape_squeeze.6
  1.5 0.7 compare_and_fusion
  2.3 3.6 gather_fusion
  5.9 0.9 broadcast_select_fusion
  6.8 10.4 %all-to-all-start = ((bf16[32,32,128]{2,1,0:T(8,128)(2,1)}), bf16[32,32,128]{2,1,0:T(8,128)(2,1)S(1)}, u32[]{:S(2)}, u32[]{:S(2)}) async-start(bf16[32,32,128]{2,1,0:T(8,128)(2,1)} %broadcast_select_fusion), calls=%async_computation | async-start | bytes 524288 | tf_op jit(solution)/shard_map/all_to_all | solution.py:122
  18.0 0.7 fusion.44
  18.7 0.7 fusion.45
  19.5 2.5 fusion.40
  22.7 0.7 multiply_convert_fusion.3
  23.4 2.8 all-to-all-done
  26.3 1.1 stack.20
  27.4 18.5 %all-to-all-start.1 = ((f32[512,4,16]{2,1,0:T(4,128)}), f32[512,4,16]{2,1,0:T(4,128)S(1)}, u32[]{:S(2)}, u32[]{:S(2)}) async-start(f32[512,4,16]{2,1,0:T(4,128)} %stack.20), calls=%async_computation.1 | async-start | bytes 2097152 | tf_op jit(solution)/shard_map/all_to_all | solution.py:142
  46.2 2.0 gather_fusion.1
  49.5 0.7 add_convert_fusion
  50.2 2.7 fusion.1
  53.2 111.5 %all-reduce = f32[8192]{0:T(1024)S(1)} all-reduce(f32[8192]{0:T(1024)S(1)} %dynamic-update-slice), channel_id=1, replica_groups=mesh['row'=16,'space'=32] {'row','space'}, use_global_device_ids=true, to_apply=%add | all-reduce | flops 8192 | bytes 65536
  164.7 0.9 fusion.19
  166.9 3.1 multiply_reduce_fusion.12
  170.1 100.5 %all-reduce.3 = (f32[]{:T(128)}, f32[]{:T(128)}) all-reduce(f32[]{:T(128)} %get-tuple-element.67, f32[]{:T(128)} %get-tuple-element.66), channel_id=1, replica_groups=mesh['row'=16,'space'=32] {'row','space'}, use_global_device_ids=true, to_apply=%region_3.4 | all-reduce | flops 2 | bytes 16 | tf_op jit(solution)/shard_map/psum | solution.py:157
  272.5 99.7 %psum.30 = f32[]{:T(128)} all-reduce(f32[]{:T(128)} %get-tuple-element.83), channel_id=1, replica_groups=mesh['row'=16,'space'=32] {'row','space'}, use_global_device_ids=true, to_apply=%region_9.10 | all-reduce | flops 1 | bytes 8 | tf_op jit(solution)/shard_map/psum | solution.py:157
  373.7 100.2 %all-reduce.1 = f32[8192]{0:T(1024)S(1)} all-reduce(f32[8192]{0:T(1024)S(1)} %get-tuple-element.81), channel_id=1, replica_groups=mesh['row'=16,'space'=32] {'row','space'}, use_global_device_ids=true, to_apply=%add.1 | all-reduce | flops 8192 | bytes 65536
  474.8 99.7 %psum.31 = f32[]{:T(128)} all-reduce(f32[]{:T(128)} %multiply_reduce_fusion.10), channel_id=1, replica_groups=mesh['row'=16,'space'=32] {'row','space'}, use_global_device_ids=true, to_apply=%region_12.13 | all-reduce | flops 1 | bytes 8 | tf_op jit(solution)/shard_map/psum | solution.py:165
  576.2 100.0 %all-reduce.2 = f32[8192]{0:T(1024)S(1)} all-reduce(f32[8192]{0:T(1024)S(1)} %dynamic-update-slice.2), channel_id=1, replica_groups=mesh['row'=16,'space'=32] {'row','space'}, use_global_device_ids=true, to_apply=%add.2 | all-reduce | flops 8192 | bytes 65536
  676.2 0.9 multiply_reduce_fusion.2
  (79 shorter events, 7.6 us)
Async XLA Ops:
  0.6 18.7 %copy-start = (bf16[128,256]{1,0:T(8,128)(2,1)S(1)}, bf16[128,256]{1,0:T(8,128)(2,1)}, u32[]{:S(2)}) copy-start(bf16[128,256]{1,0:T(8,128)(2,1)} %param.23) | copy-start | bytes 196612
  2.2 15.0 %copy-start.6 = (s32[512]{0:T(512)S(1)}, s32[512]{0:T(512)}, u32[]{:S(2)}) copy-start(s32[512]{0:T(512)} %param.21) | copy-start | bytes 6148
  2.2 15.1 %copy-start.4 = (f32[3,512]{1,0:T(4,128)S(1)}, f32[3,512]{1,0:T(4,128)}, u32[]{:S(2)}) copy-start(f32[3,512]{1,0:T(4,128)} %param.22) | copy-start | bytes 18436
  2.2 15.1 %copy-start.7 = (f32[4]{0:T(128)S(1)}, f32[4]{0:T(128)}, u32[]{:S(2)}) copy-start(f32[4]{0:T(128)} %param.28) | copy-start | bytes 52
  2.3 15.7 %copy-start.8 = (f32[4]{0:T(128)S(1)}, f32[4]{0:T(128)}, u32[]{:S(2)}) copy-start(f32[4]{0:T(128)} %param.29) | copy-start | bytes 52
  2.3 16.4 %copy-start.9 = (f32[4]{0:T(128)S(1)}, f32[4]{0:T(128)}, u32[]{:S(2)}) copy-start(f32[4]{0:T(128)} %param.30) | copy-start | bytes 52
  2.3 17.1 %copy-start.1 = (bf16[16,128]{1,0:T(8,128)(2,1)S(1)}, bf16[16,128]{1,0:T(8,128)(2,1)}, u32[]{:S(2)}) copy-start(bf16[16,128]{1,0:T(8,128)(2,1)} %param.16) | copy-start | bytes 12292
  2.3 17.2 %copy-start.10 = (s32[16]{0:T(128)S(1)}, s32[16]{0:T(128)}, u32[]{:S(2)}) copy-start(s32[16]{0:T(128)} %param.18) | copy-start | bytes 196
  2.3 19.7 %copy-start.5 = (f32[3,16]{1,0:T(4,128)S(1)}, f32[3,16]{1,0:T(4,128)}, u32[]{:S(2)}) copy-start(f32[3,16]{1,0:T(4,128)} %param.17) | copy-start | bytes 580
  2.3 20.4 %copy-start.12 = (f32[8,128]{1,0:T(8,128)S(1)}, f32[8,128]{1,0:T(8,128)}, u32[]{:S(2)}) copy-start(f32[8,128]{1,0:T(8,128)} %param.24) | copy-start | bytes 12292
  6.8 19.4 %all-to-all-start = ((bf16[32,32,128]{2,1,0:T(8,128)(2,1)}), bf16[32,32,128]{2,1,0:T(8,128)(2,1)S(1)}, u32[]{:S(2)}, u32[]{:S(2)}) async-start(bf16[32,32,128]{2,1,0:T(8,128)(2,1)} %broadcast_select_fusion), calls=%async_computation | async-start | bytes 524288 | tf_op jit(solution)/shard_map/all_to_all | solution.py:122
  27.4 137.3 %all-to-all-start.1 = ((f32[512,4,16]{2,1,0:T(4,128)}), f32[512,4,16]{2,1,0:T(4,128)S(1)}, u32[]{:S(2)}, u32[]{:S(2)}) async-start(f32[512,4,16]{2,1,0:T(4,128)} %stack.20), calls=%async_computation.1 | async-start | bytes 2097152 | tf_op jit(solution)/shard_map/all_to_all | solution.py:142
  46.2 2.1 copy-start.2
  48.2 0.7 copy-start.13
  48.6 0.8 copy-start.3
  48.6 1.6 copy-start.14
  575.9 101.7 %copy-start.11 = (f32[16]{0:T(128)}, f32[16]{0:T(128)S(1)}, u32[]{:S(2)}) copy-start(f32[16]{0:T(128)S(1)} %get-tuple-element.71) | copy-start | bytes 196
